TPU v7x, 32 devices: a whole 2x2x4 slice. The times are simulated.
32 devices in a mesh: tile: 4 (over y, core), rep: 8 (over z, x).
Axes of the slice: x: 2, y: 2, z: 4, core: 2. Of those that a mesh axis runs over, the one named last changes fastest.
Arguments:
- inputs: bfloat16 [8, 8, 32, 32, 256], P('rep', 'tile'), may hold values from -6 to 6
- grad_out: bfloat16 [8, 8, 32, 32, 256], P('rep', 'tile'), may hold values from -6 to 6
- seam_links: int32 [8, 4, 3], P('tile'), may hold values from 0 to 7, as said below
- corner_links: int32 [8, 4, 2], P('tile'), may hold values from 0 to 7, as said below
- dw_weight: float32 [256, 9], replicated, may hold values from -1 to 1
- norm_gain: float32 [256], replicated, may hold values from 0.1 to 1.9
- w_in: bfloat16 [256, 1024], replicated, may hold values from -0.375 to 0.375
- bias_in: float32 [1024], replicated, may hold values from -1 to 1
- w_out: bfloat16 [1024, 256], replicated, may hold values from -0.1875 to 0.1875
- layer_scale: float32 [256], replicated, may hold values from 0.25 to 2
Outputs:
- block_out: bfloat16 [8, 8, 32, 32, 256], P('rep', 'tile')
- x_grad: float32 [8, 8, 32, 32, 256], P('rep', 'tile')
- grad_dw: float32 [256, 9], replicated
- grad_gain: float32 [256], replicated
- grad_w_in: float32 [256, 1024], replicated
- grad_bias: float32 [1024], replicated
- grad_w_out: float32 [1024, 256], replicated
- grad_scale: float32 [256], replicated
Inputs may be any that keep to these rules, and one draw needn't show every extreme that they name: `seam_links`: entry [t, s] = (t2, s2, f): side s of tile t meets side s2 of tile t2, reversed if f = 1. Sides are paired: entry [t2, s2] = (t, s, f), and no entry names its own side. `corner_links`: entry [t, k] = (t2, k2): corner k of tile t meets corner k2 of tile t2. Corners are paired: entry [t2, k2] = (t, k), and no entry names its own corner.
All inputs are finite; a program needn't handle non-finite values.
Results may differ from a plain program's by a relative error of at most 0.0063.
Values may be sent and summed in bfloat16 or wider, within the bound.
A program may use at most 64 MiB of HBM per device.

v0:
```python
import math
import jax
import jax.numpy as jnp
from jax import lax
from jax.sharding import PartitionSpec as P

INV_ROOT_TWO = 0.7071067811865476
INV_ROOT_TAU = 0.3989422804014327


def edge_strips(blocks):
    top_row = blocks[..., 0, :, :]
    right_col = blocks[..., :, -1, :]
    bottom_row = blocks[..., -1, ::-1, :]
    left_col = blocks[..., ::-1, 0, :]
    return jnp.stack([top_row, right_col, bottom_row, left_col], axis=-3)


def corner_cells(blocks):
    return jnp.stack(
        [
            blocks[..., 0, 0, :],
            blocks[..., 0, -1, :],
            blocks[..., -1, -1, :],
            blocks[..., -1, 0, :],
        ],
        axis=-2,
    )


def fetch_linked(all_strips, all_points, seam_links, corner_links):
    picked = all_strips[:, seam_links[..., 0], seam_links[..., 1]]
    reverse = (seam_links[..., 2] == 1)[None, :, :, None, None]
    strips = jnp.where(reverse, picked[..., ::-1, :], picked)
    points = all_points[:, corner_links[..., 0], corner_links[..., 1]]
    return (strips, points)


def assemble(blocks, strips, points):
    top_row = jnp.concatenate(
        [points[..., 0:1, :], strips[..., 0, :, :], points[..., 1:2, :]], axis=-2
    )
    bottom_row = jnp.concatenate(
        [points[..., 3:4, :], strips[..., 2, ::-1, :], points[..., 2:3, :]], axis=-2
    )
    left_col = strips[..., 3, ::-1, :][..., :, None, :]
    right_col = strips[..., 1, :, :][..., :, None, :]
    middle = jnp.concatenate([left_col, blocks, right_col], axis=-2)
    return jnp.concatenate([top_row[..., None, :, :], middle, bottom_row[..., None, :, :]], axis=-3)


def padded_parts(grad_padded):
    interior = grad_padded[..., 1:-1, 1:-1, :]
    top_row = grad_padded[..., 0, 1:-1, :]
    right_col = grad_padded[..., 1:-1, -1, :]
    bottom_row = grad_padded[..., -1, 1:-1, :][..., ::-1, :]
    left_col = grad_padded[..., 1:-1, 0, :][..., ::-1, :]
    strips = jnp.stack([top_row, right_col, bottom_row, left_col], axis=-3)
    points = jnp.stack(
        [
            grad_padded[..., 0, 0, :],
            grad_padded[..., 0, -1, :],
            grad_padded[..., -1, -1, :],
            grad_padded[..., -1, 0, :],
        ],
        axis=-2,
    )
    return (interior, strips, points)


def add_to_rims(target, strips, points):
    extent = target.shape[-2]
    row_ids = lax.broadcasted_iota(jnp.int32, (extent, 1, 1), 0)
    col_ids = lax.broadcasted_iota(jnp.int32, (1, extent, 1), 1)
    top_mask = row_ids == 0
    bottom_mask = row_ids == extent - 1
    left_mask = col_ids == 0
    right_mask = col_ids == extent - 1
    target = target + jnp.where(top_mask, strips[..., 0, :, :][..., None, :, :], 0.0)
    target = target + jnp.where(right_mask, strips[..., 1, :, :][..., :, None, :], 0.0)
    target = target + jnp.where(bottom_mask, strips[..., 2, ::-1, :][..., None, :, :], 0.0)
    target = target + jnp.where(left_mask, strips[..., 3, ::-1, :][..., :, None, :], 0.0)
    target = target + jnp.where(top_mask & left_mask, points[..., 0, :][..., None, None, :], 0.0)
    target = target + jnp.where(top_mask & right_mask, points[..., 1, :][..., None, None, :], 0.0)
    target = target + jnp.where(
        bottom_mask & right_mask, points[..., 2, :][..., None, None, :], 0.0
    )
    target = target + jnp.where(bottom_mask & left_mask, points[..., 3, :][..., None, None, :], 0.0)
    return target


def forward_backward(
    padded, blocks, grad_out, dw_weight, norm_gain, w_in, bias_in, w_out, layer_scale
):
    extent = blocks.shape[-2]
    channels = blocks.shape[-1]
    mixed_cells = jnp.zeros(blocks.shape, jnp.float32)
    for row_off in range(3):
        for col_off in range(3):
            tap_index = 3 * row_off + col_off
            window = padded[..., row_off : row_off + extent, col_off : col_off + extent, :].astype(
                jnp.float32
            )
            mixed_cells = mixed_cells + window * dw_weight[:, tap_index]
    average = jnp.mean(mixed_cells, axis=-1, keepdims=True)
    centred = mixed_cells - average
    inv_std = lax.rsqrt(jnp.mean(centred * centred, axis=-1, keepdims=True) + 1e-06)
    standard = centred * inv_std
    normed = (standard * norm_gain).astype(jnp.bfloat16).reshape(-1, channels)
    hidden_pre = jnp.dot(normed, w_in, preferred_element_type=jnp.float32) + bias_in
    activated = jax.nn.gelu(hidden_pre, approximate=False).astype(jnp.bfloat16)
    branch = jnp.dot(activated, w_out, preferred_element_type=jnp.float32)
    cotangent = grad_out.reshape(-1, channels).astype(jnp.float32)
    block_out = (
        (blocks.reshape(-1, channels).astype(jnp.float32) + layer_scale * branch)
        .astype(jnp.bfloat16)
        .reshape(blocks.shape)
    )
    grad_scale = jnp.sum(cotangent * branch, axis=0)
    grad_mix = (cotangent * layer_scale).astype(jnp.bfloat16)
    grad_w_out = lax.dot_general(
        activated, grad_mix, (((0,), (0,)), ((), ())), preferred_element_type=jnp.float32
    )
    grad_act = lax.dot_general(
        grad_mix, w_out, (((1,), (1,)), ((), ())), preferred_element_type=jnp.float32
    )
    gelu_slope = (
        0.5 * (1.0 + lax.erf(hidden_pre * INV_ROOT_TWO))
        + hidden_pre * jnp.exp(-0.5 * hidden_pre * hidden_pre) * INV_ROOT_TAU
    )
    grad_hidden = (grad_act * gelu_slope).astype(jnp.bfloat16)
    grad_bias = jnp.sum(grad_hidden.astype(jnp.float32), axis=0)
    grad_w_in = lax.dot_general(
        normed, grad_hidden, (((0,), (0,)), ((), ())), preferred_element_type=jnp.float32
    )
    grad_normed = lax.dot_general(
        grad_hidden, w_in, (((1,), (1,)), ((), ())), preferred_element_type=jnp.float32
    ).reshape(blocks.shape)
    grad_gain = jnp.sum((grad_normed * standard).reshape(-1, channels), axis=0)
    grad_unit = grad_normed * norm_gain
    grad_mixed = (
        grad_unit
        - jnp.mean(grad_unit, axis=-1, keepdims=True)
        - standard * jnp.mean(grad_unit * standard, axis=-1, keepdims=True)
    ) * inv_std
    pad_widths = [(0, 0)] * (grad_mixed.ndim - 3) + [(2, 2), (2, 2), (0, 0)]
    wide_grad = jnp.pad(grad_mixed, pad_widths)
    grad_padded = jnp.zeros(padded.shape, jnp.float32)
    dw_columns = []
    for row_off in range(3):
        for col_off in range(3):
            tap_index = 3 * row_off + col_off
            window = padded[..., row_off : row_off + extent, col_off : col_off + extent, :].astype(
                jnp.float32
            )
            shifted = wide_grad[
                ..., 2 - row_off : 4 - row_off + extent, 2 - col_off : 4 - col_off + extent, :
            ]
            grad_padded = grad_padded + shifted * dw_weight[:, tap_index]
            dw_columns.append(jnp.sum((grad_mixed * window).reshape(-1, channels), axis=0))
    grad_dw = jnp.stack(dw_columns, axis=1)
    return (
        block_out,
        grad_padded,
        (grad_dw, grad_gain, grad_w_in, grad_bias, grad_w_out, grad_scale),
    )


def body(
    inputs,
    grad_out,
    seam_links,
    corner_links,
    dw_weight,
    norm_gain,
    w_in,
    bias_in,
    w_out,
    layer_scale,
):
    all_strips, all_points = (
        lax.all_gather(edge_strips(inputs), "tile", axis=1, tiled=True),
        lax.all_gather(corner_cells(inputs), "tile", axis=1, tiled=True),
    )
    strips, points = fetch_linked(all_strips, all_points, seam_links, corner_links)
    padded = assemble(inputs, strips, points)
    block_out, grad_padded, partials = forward_backward(
        padded, inputs, grad_out, dw_weight, norm_gain, w_in, bias_in, w_out, layer_scale
    )
    grad_dw, grad_gain, grad_w_in, grad_bias, grad_w_out, grad_scale = partials
    interior, back_strips, back_points = padded_parts(grad_padded)
    home_strips, home_points = (
        lax.all_gather(back_strips.astype(jnp.bfloat16), "tile", axis=1, tiled=True).astype(
            back_strips.dtype
        ),
        lax.all_gather(back_points.astype(jnp.bfloat16), "tile", axis=1, tiled=True).astype(
            back_points.dtype
        ),
    )
    return_strips, return_points = fetch_linked(home_strips, home_points, seam_links, corner_links)
    x_grad = add_to_rims(grad_out.astype(jnp.float32) + interior, return_strips, return_points)
    cell_total = (
        lax.axis_size("tile")
        * lax.axis_size("rep")
        * inputs.shape[0]
        * inputs.shape[1]
        * inputs.shape[2]
        * inputs.shape[3]
    )
    factor = 1.0 / math.sqrt(cell_total)
    summed = lax.psum(
        (grad_dw, grad_gain, grad_w_in, grad_bias, grad_w_out, grad_scale), ("tile", "rep")
    )
    return (
        block_out,
        x_grad,
        summed[0] * factor,
        summed[1] * factor,
        summed[2] * factor,
        summed[3] * factor,
        summed[4] * factor,
        summed[5] * factor,
    )


def solution(mesh):
    placed = (
        P("rep", "tile", None, None, None),
        P("rep", "tile", None, None, None),
        P("tile", None, None),
        P("tile", None, None),
        P(),
        P(),
        P(),
        P(),
        P(),
        P(),
    )
    return jax.shard_map(
        body,
        mesh=mesh,
        in_specs=placed,
        out_specs=(
            P("rep", "tile", None, None, None),
            P("rep", "tile", None, None, None),
            P(),
            P(),
            P(),
            P(),
            P(),
            P(),
        ),
        check_vma=False,
    )
```

profile of v0, /device:TPU:0, one launch (start us, length us, event | category | flops | bytes accessed | tf_op | source)
XLA Modules:
  0.0 216.6 jit_solution(4268885214619424398)
XLA Ops:
  7.3 0.9 fusion.76
  8.1 1.1 fusion.75
  9.3 0.8 slice_bitcast_fusion.8
  11.5 6.2 %all_gather.12 = bf16[1,8,4,256]{3,2,0,1:T(4,128)(2,1)S(1)} all-gather(bf16[1,2,4,256]{3,2,0,1:T(4,128)(2,1)S(1)} %copy.212), channel_id=1, replica_groups=mesh['tile'=4,'rep'=8] {'tile'}, dimensions={1}, use_global_device_ids=true | all-gather | bytes 20480 | tf_op jit(solution)/shard_map/all_gather | solution.py:183
  17.7 0.8 fusion.71
  19.4 7.6 %all_gather.13 = bf16[1,8,4,32,256]{4,3,1,2,0:T(8,128)(2,1)S(1)} all-gather(bf16[1,2,4,32,256]{4,3,1,2,0:T(8,128)(2,1)S(1)} %pad_maximum_fusion.3), channel_id=1, replica_groups=mesh['tile'=4,'rep'=8] {'tile'}, dimensions={1}, use_global_device_ids=true | all-gather | bytes 655360 | tf_op jit(solution)/shard_map/all_gather | solution.py:182
  28.4 1.7 maximum_maximum_fusion
  30.1 5.2 %fusion.72 = (f32[2,32,32]{2,1,0:T(8,128)S(1)}, f32[1,2,32,32,256]{4,3,2,1,0:T(8,128)S(1)}) fusion(f32[256]{0:T(256)S(1)} %bitcast.170, bf16[1,2,33,34,256]{4,3,2,1,0:T(8,128)(2,1)S(1)} %get-tuple-element.81, f32[256]{0:T(256)S(1)} %bitcast.172, f32[256]{0:T(256)S(1)} %bitcast.158, f32[256]{0:T(256)S(1)} %bitcast.160, ...), kind=kLoop, calls=%fused_computation.185 | loop fusion | flops 17299456 | bytes 9520128 | tf_op jit(solution)/shard_map/reduce_sum | solution.py:105
  36.0 0.7 multiply_convert_fusion
  36.8 19.3 %fusion.2 = (bf16[2048,1024]{1,0:T(8,128)(2,1)S(1)}, f32[2048,1024]{1,0:T(8,128)S(1)}) fusion(f32[1024]{0:T(1024)S(1)} %copy-done.13, bf16[2048,256]{1,0:T(8,128)(2,1)S(1)} %bitcast.144, bf16[256,1024]{1,0:T(8,128)(2,1)S(1)} %copy-done), kind=kOutput, calls=%fused_computation.8 | convolution fusion | flops 1212153856 | bytes 14159872 | tf_op jit(solution)/shard_map/dot_general | solution.py:110
  56.2 3.1 %fusion.58 = (f32[256]{0:T(256)}, bf16[2048,256]{1,0:T(8,128)(2,1)}, bf16[2048,256]{1,0:T(8,128)(2,1)S(1)}) fusion(bf16[1,2,32,32,256]{4,3,2,1,0:T(8,128)(2,1)S(1)} %copy-done.6, f32[256]{0:T(256)S(1)} %copy-done.14, bf16[1,2,32,32,256]{4,3,2,1,0:T(8,128)(2,1)S(1)} %copy-done.5, bf16[2048,1024]{1,0:T(8,128)(2,1)S(1)} %get-tuple-element.122, ...), kind=kOutput, calls=%fused_computation.102 | convolution fusion | flops 1078460160 | bytes 8914944 | tf_op jit(solution)/shard_map/dot_general | solution.py:112
  59.3 2.2 %fusion.82 = f32[1024,256]{1,0:T(8,128)} fusion(bf16[2048,1024]{1,0:T(8,128)(2,1)S(1)} %get-tuple-element.122, bf16[2048,256]{1,0:T(8,128)(2,1)S(1)} %get-tuple-element.82), kind=kOutput, calls=%fused_computation.194 | convolution fusion | flops 1073741824 | bytes 6291456 | tf_op jit(solution)/shard_map/dot_general | solution.py:121
  61.5 4.9 %convert_reduce_fusion = (f32[1024]{0:T(1024)S(1)}, bf16[2048,1024]{1,0:T(8,128)(2,1)S(1)}) fusion(f32[2048,1024]{1,0:T(8,128)S(1)} %get-tuple-element.123, f32[1024]{0:T(1024)S(1)} %copy-done.13, bf16[2048,256]{1,0:T(8,128)(2,1)S(1)} %get-tuple-element.82, bf16[1024,256]{1,0:T(8,128)(2,1)S(1)} %copy-done.12), kind=kOutput, calls=%fused_computation.15 | convolution fusion | flops 1101003776 | bytes 14163968 | tf_op jit(solution)/shard_map/dot_general | solution.py:124
  66.4 1.9 copy-done.15
  68.3 2.2 %fusion.81 = f32[256,1024]{1,0:T(8,128)} fusion(bf16[2048,256]{1,0:T(8,128)(2,1)S(1)} %bitcast.145, bf16[2048,1024]{1,0:T(8,128)(2,1)S(1)} %get-tuple-element.127), kind=kOutput, calls=%fused_computation.193 | convolution fusion | flops 1073741824 | bytes 6291456 | tf_op jit(solution)/shard_map/dot_general | solution.py:133
  70.6 3.6 %multiply_reduce_fusion.3 = (f32[2048]{0:T(1024)S(1)}, f32[2048,256]{1,0:T(8,128)S(1)}) fusion(f32[256]{0:T(256)S(1)} %copy-done.9, bf16[2048,1024]{1,0:T(8,128)(2,1)} %copy-done.15, bf16[256,1024]{1,0:T(8,128)(2,1)S(1)} %copy-done), kind=kOutput, calls=%fused_computation.109 | convolution fusion | flops 1074788352 | bytes 6824960 | tf_op jit(solution)/shard_map/dot_general | solution.py:136
  74.2 1.1 multiply_reduce_fusion
  75.6 8.3 %fusion.48 = (f32[256]{0:T(256)S(1)}, f32[256]{0:T(256)S(1)}, f32[256]{0:T(256)S(1)}, f32[256]{0:T(256)S(1)}, f32[256]{0:T(256)S(1)}, /*index=5*/f32[256]{0:T(25...) fusion(bf16[1,2,33,34,256]{4,3,2,1,0:T(8,128)(2,1)} %copy-done.2, ...), kind=kLoop, calls=%fused_computation.89 | loop fusion | flops 20969216 | bytes 13740032 | tf_op jit(solution)/shard_map/reduce_sum | solution.py:160
  83.9 2.8 %fusion.24 = f32[1,2,34,34,256]{4,3,2,1,0:T(8,128)S(1)} fusion(f32[1,2,32,32,256]{4,3,2,1,0:T(8,128)S(1)} %get-tuple-element.71, f32[256]{0:T(256)S(1)} %bitcast.171, f32[256]{0:T(256)S(1)} %bitcast.173, f32[256]{0:T(256)S(1)} %bitcast.159, f32[256]{0:T(256)S(1)} %bitcast.161, f32[256]{0:T(256)S(1)} %bitcast.163, f32[256]{0:T(256)S(1)} %bitcast.165, ...), kind=kLoop, calls=%fused_computation.48 | loop fusion | flops 10061824 | bytes 4473856 | tf_op jit(solution)/shard_map/add | solution.py:159
  88.7 40.9 %all-reduce.1 = (f32[256,9]{0,1:T(8,128)}, f32[256]{0:T(256)S(1)}, f32[1024]{0:T(1024)S(1)}, f32[256]{0:T(256)S(1)}) all-reduce(f32[256,9]{0,1:T(8,128)S(1)} %stack.78, f32[256]{0:T(256)S(1)} %get-tuple-element.57, f32[1024]{0:T(1024)S(1)} %get-tuple-element.126, ...), channel_id=1, replica_groups=mesh['tile'=4,'rep'=8] {'tile','rep'}, use_global_device_ids=true, to_apply=%region_13.14 | all-reduce | flops 3840 | bytes 30720 | tf_op jit(solution)/shard_map/psum | solution.py:211
  131.6 0.8 pad_maximum_fusion.4
  132.4 8.5 %all_gather.14 = bf16[1,8,4,32,256]{4,3,2,0,1:T(8,128)(2,1)S(1)} all-gather(bf16[1,2,4,32,256]{4,3,2,0,1:T(8,128)(2,1)S(1)} %copy.228), channel_id=1, replica_groups=mesh['tile'=4,'rep'=8] {'tile'}, dimensions={1}, use_global_device_ids=true | all-gather | bytes 655360 | tf_op jit(solution)/shard_map/all_gather | solution.py:193
  140.9 1.1 bitcast_convert_fusion
  142.0 2.5 %gather_fusion.2 = f32[8,32,256]{2,1,0:T(8,128)} fusion(f32[8,4,32,256]{3,2,1,0:T(8,128)} %bitcast_convert_fusion, s32[8]{0:T(128)S(1)} %reshape.484), kind=kCustom, calls=%fused_computation.2 | custom fusion | bytes 524352 | tf_op jit(solution)/shard_map/gather | solution.py:32
  144.5 1.6 rev.37
  146.1 1.1 broadcast_select_fusion
  148.6 5.2 %all_gather.15 = bf16[1,8,4,256]{3,2,0,1:T(4,128)(2,1)S(1)} all-gather(bf16[1,2,4,256]{3,2,0,1:T(4,128)(2,1)S(1)} %copy.230), channel_id=1, replica_groups=mesh['tile'=4,'rep'=8] {'tile'}, dimensions={1}, use_global_device_ids=true | all-gather | bytes 20480 | tf_op jit(solution)/shard_map/all_gather | solution.py:196
  154.5 0.8 rev.39
  156.0 4.5 %fusion.56 = f32[1,2,32,32,256]{4,3,2,1,0:T(8,128)} fusion(f32[1,2,34,34,256]{4,3,2,1,0:T(8,128)S(1)} %fusion.24, bf16[1,2,32,32,256]{4,3,2,1,0:T(8,128)(2,1)} %param.11, f32[2,256]{1,0:T(2,128)S(1)} %bitcast.174, f32[2,256]{1,0:T(2,128)S(1)} %bitcast.175, f32[2,256]{1,0:T(2,128)S(1)} %bitcast.176, f32[2,256]{1,0:T(2,128)S(1)} %bitcast.177, ...), kind=kLoop, calls=%fused_computation.98 | loop fusion | flops 9437184 | bytes 5531648 | tf_op jit(solution)/shard_map/add | solution.py:88
  160.5 45.8 %all-reduce.5.cloned.1.call-done = (f32[256,1024]{1,0:T(8,128)}, f32[1024,256]{1,0:T(8,128)}) async-done(((f32[256,1024]{1,0:T(8,128)}, f32[1024,256]{1,0:T(8,128)}), (f32[256,1024]{1,0:T(8,128)}, f32[1024,256]{1,0:T(8,128)})) %all-reduce.5.cloned.1.call-update) | async-done | bytes 2097168 | tf_op jit(solution)/shard_map/psum | solution.py:211
  206.3 2.4 %broadcast_multiply_fusion = f32[1024,256]{1,0:T(8,128)} fusion(f32[1024,256]{1,0:T(8,128)} %get-tuple-element.70), kind=kLoop, calls=%fused_computation.118 | loop fusion | flops 262144 | bytes 2097152 | tf_op jit(solution)/shard_map/mul | solution.py:221
  208.6 1.1 broadcast_multiply_fusion.1
  (101 shorter events, 11.2 us)
Async XLA Ops:
  7.2 29.6 %copy-start = (bf16[256,1024]{1,0:T(8,128)(2,1)S(1)}, bf16[256,1024]{1,0:T(8,128)(2,1)}, u32[]{:S(2)}) copy-start(bf16[256,1024]{1,0:T(8,128)(2,1)} %param.16) | copy-start | bytes 1572868
  7.2 21.2 %copy-start.4 = (bf16[1,2,32,32,256]{4,3,2,1,0:T(8,128)(2,1)S(1)}, bf16[1,2,32,32,256]{4,3,2,1,0:T(8,128)(2,1)}, u32[]{:S(2)}) copy-start(bf16[1,2,32,32,256]{4,3,2,1,0:T(8,128)(2,1)} %param.10) | copy-start | bytes 3145732
  7.2 21.1 %copy-start.10 = (f32[256,9]{0,1:T(8,128)S(1)}, f32[256,9]{0,1:T(8,128)}, u32[]{:S(2)}) copy-start(f32[256,9]{0,1:T(8,128)} %param.14) | copy-start | bytes 27652
  7.2 199.1 %all-reduce.5.cloned.1.call-start = ((), (), s32[]{:S(2)}) async-start(), calls=%async_computation | async-start | bytes 4194304 | tf_op jit(solution)/shard_map/psum | solution.py:211
  11.4 16.4 %copy-start.11 = (pred[2,4]{1,0:T(4,128)(4,1)}, pred[2,4]{1,0:T(4,128)(4,1)S(1)}, u32[]{:S(2)}) copy-start(pred[2,4]{1,0:T(4,128)(4,1)S(1)} %compare_bitcast_fusion) | copy-start | bytes 28
  30.1 5.2 %copy-start.1 = (bf16[1,2,33,34,256]{4,3,2,1,0:T(8,128)(2,1)}, bf16[1,2,33,34,256]{4,3,2,1,0:T(8,128)(2,1)S(1)}, u32[]{:S(2)}) copy-start(bf16[1,2,33,34,256]{4,3,2,1,0:T(8,128)(2,1)S(1)} %get-tuple-element.80) | copy-start | bytes 3446788
  30.1 5.2 %copy-start.2 = (bf16[1,2,33,34,256]{4,3,2,1,0:T(8,128)(2,1)}, bf16[1,2,33,34,256]{4,3,2,1,0:T(8,128)(2,1)S(1)}, u32[]{:S(2)}) copy-start(bf16[1,2,33,34,256]{4,3,2,1,0:T(8,128)(2,1)S(1)} %get-tuple-element.81) | copy-start | bytes 3446788
  30.1 5.9 %copy-start.9 = (f32[256]{0:T(256)S(1)}, f32[256]{0:T(256)}, u32[]{:S(2)}) copy-start(f32[256]{0:T(256)} %param.15) | copy-start | bytes 3076
  35.3 1.4 copy-start.13
  36.8 19.4 %copy-start.5 = (bf16[1,2,32,32,256]{4,3,2,1,0:T(8,128)(2,1)S(1)}, bf16[1,2,32,32,256]{4,3,2,1,0:T(8,128)(2,1)}, u32[]{:S(2)}) copy-start(bf16[1,2,32,32,256]{4,3,2,1,0:T(8,128)(2,1)} %param.10) | copy-start | bytes 3145732
  36.8 19.4 %copy-start.6 = (bf16[1,2,32,32,256]{4,3,2,1,0:T(8,128)(2,1)S(1)}, bf16[1,2,32,32,256]{4,3,2,1,0:T(8,128)(2,1)}, u32[]{:S(2)}) copy-start(bf16[1,2,32,32,256]{4,3,2,1,0:T(8,128)(2,1)} %param.11) | copy-start | bytes 3145732
  36.8 19.4 %copy-start.12 = (bf16[1024,256]{1,0:T(8,128)(2,1)S(1)}, bf16[1024,256]{1,0:T(8,128)(2,1)}, u32[]{:S(2)}) copy-start(bf16[1024,256]{1,0:T(8,128)(2,1)} %param.18) | copy-start | bytes 1572868
  36.8 19.4 %copy-start.14 = (f32[256]{0:T(256)S(1)}, f32[256]{0:T(256)}, u32[]{:S(2)}) copy-start(f32[256]{0:T(256)} %param.19) | copy-start | bytes 3076
  66.4 1.9 copy-start.15
  74.2 1.3 copy-start.3
  132.3 23.1 %copy-start.8 = (f32[256,9]{0,1:T(8,128)S(1)}, f32[256,9]{0,1:T(8,128)}, u32[]{:S(2)}) copy-start(f32[256,9]{0,1:T(8,128)} %get-tuple-element.65) | copy-start | bytes 27652
  206.3 2.4 %copy-start.7 = (f32[256,1024]{1,0:T(8,128)S(1)}, f32[256,1024]{1,0:T(8,128)}, u32[]{:S(2)}) copy-start(f32[256,1024]{1,0:T(8,128)} %get-tuple-element.69) | copy-start | bytes 3145732
Sparse Core Ops, SparseCore 0:
  70.7 135.4 all-reduce.4
where the time goes:
time: 217 us
  blocking collectives  68.5 us (32%)
  waiting for transfers between devices  45.8 us (21%)
  other arithmetic  35.4 us (16%)
  matrix products  35.4 us (16%)
  local copies, waits for them, and re-layouts  16.8 us (8%)
  between operations  14.6 us (7%)
    psum x1, waiting for transfers between devices, body(): lax.psum((grad_dw, grad_gain, grad_w_in, grad_bias, grad_w_out, grad_scal...  45.8 us
    psum x1, blocking collectives, body(): lax.psum((grad_dw, grad_gain, grad_w_in, grad_bias, grad_w_out, grad_scal...  40.9 us
    dot_general x1, matrix products, forward_backward(): jnp.dot(normed, w_in, preferred_element_type=jnp.float32) + bias_in  19.3 us
    all_gather x1, blocking collectives, body(): lax.all_gather(back_strips.astype(jnp.bfloat16), 'tile', axis=1, tiled=True)  8.53 us
    reduce_sum x1, other arithmetic, forward_backward(): jnp.sum((grad_mixed * window).reshape(-1, channels), axis=0)  8.32 us
    all_gather x1, blocking collectives, body(): lax.all_gather(edge_strips(inputs), 'tile', axis=1, tiled=True)  7.62 us
    all_gather x1, blocking collectives, body(): lax.all_gather(corner_cells(inputs), 'tile', axis=1, tiled=True)  6.22 us
    all_gather x1, blocking collectives, body(): lax.all_gather(back_points.astype(jnp.bfloat16), 'tile', axis=1, tiled=True)  5.19 us
  transfers between devices with their start and end apart: 1, of which 1 were waited for; matrix products, arithmetic and copies ran while one was open for 16% of the time, Pallas kernels for 0%

commit v1 on v0

--- a/solution.py
+++ b/solution.py
@@ -6,6 +6,11 @@
 
 INV_ROOT_TWO = 0.7071067811865476
 INV_ROOT_TAU = 0.3989422804014327
+
+
+def by_each_axis(value, axis_one, axis_two):
+    partial = lax.psum(value, axis_one)
+    return lax.psum(partial, axis_two)
 
 
 def edge_strips(blocks):
@@ -208,8 +213,8 @@
         * inputs.shape[3]
     )
     factor = 1.0 / math.sqrt(cell_total)
-    summed = lax.psum(
-        (grad_dw, grad_gain, grad_w_in, grad_bias, grad_w_out, grad_scale), ("tile", "rep")
+    summed = by_each_axis(
+        (grad_dw, grad_gain, grad_w_in, grad_bias, grad_w_out, grad_scale), "rep", "tile"
     )
     return (
         block_out,

time: 217 us -> 240 us (1.11)
  waiting for transfers between devices: 45.8 us -> 60.4 us
  blocking collectives: 68.5 us -> 75.3 us
    psum x1 -> x2, waiting for transfers between devices: 45.8 us -> 60.4 us  [the longest x1 47.7 us: by_each_axis(): return lax.psum(partial, axis_two)]
    psum x1 -> x2, blocking collectives: 40.9 us -> 49 us  [the longest x1 38.4 us: by_each_axis(): partial = lax.psum(value, axis_one)]
  transfers between devices with their start and end apart: 1 -> 2, of which waited for: 1 -> 2; matrix products, arithmetic and copies ran while one was open for 16% -> 14% of each run, Pallas kernels for 0% -> 0%
where the time goes in v1:
time: 240 us; the launch traced here: 239 us
  blocking collectives  75.3 us (31%)
  waiting for transfers between devices  60.4 us (25%)
  matrix products  36 us (15%)
  other arithmetic  35.3 us (15%)
  local copies, waits for them, and re-layouts  17.5 us (7%)
  between operations  14.7 us (6%)
    psum x1, waiting for transfers between devices, by_each_axis(): return lax.psum(partial, axis_two)  47.7 us
    psum x1, blocking collectives, by_each_axis(): partial = lax.psum(value, axis_one)  38.4 us
    dot_general x1, matrix products, forward_backward(): jnp.dot(normed, w_in, preferred_element_type=jnp.float32) + bias_in  19.3 us
    psum x1, waiting for transfers between devices, by_each_axis(): partial = lax.psum(value, axis_one)  12.7 us
    psum x1, blocking collectives, by_each_axis(): return lax.psum(partial, axis_two)  10.6 us
    reduce_sum x1, other arithmetic, forward_backward(): jnp.sum((grad_mixed * window).reshape(-1, channels), axis=0)  8.94 us
    all_gather x1, blocking collectives, body(): lax.all_gather(edge_strips(inputs), 'tile', axis=1, tiled=True)  7.62 us
    all_gather x1, blocking collectives, body(): lax.all_gather(back_strips.astype(jnp.bfloat16), 'tile', axis=1, tiled=True)  7.29 us
  transfers between devices with their start and end apart: 2, of which 2 were waited for; matrix products, arithmetic and copies ran while one was open for 14% of the time, Pallas kernels for 0%

profile of v1, /device:TPU:0, one launch (start us, length us, event | category | flops | bytes accessed | tf_op | source)
XLA Modules:
  0.0 239.2 jit_solution(7799515082291476928)
XLA Ops:
  7.3 0.9 fusion.76
  8.1 1.1 fusion.75
  9.3 0.8 slice_bitcast_fusion.8
  11.5 6.2 %all_gather.12 = bf16[1,8,4,256]{3,2,0,1:T(4,128)(2,1)S(1)} all-gather(bf16[1,2,4,256]{3,2,0,1:T(4,128)(2,1)S(1)} %copy.212), channel_id=1, replica_groups=mesh['tile'=4,'rep'=8] {'tile'}, dimensions={1}, use_global_device_ids=true | all-gather | bytes 20480 | tf_op jit(solution)/shard_map/all_gather | solution.py:188
  19.4 7.6 %all_gather.13 = bf16[1,8,4,32,256]{4,3,1,2,0:T(8,128)(2,1)S(1)} all-gather(bf16[1,2,4,32,256]{4,3,1,2,0:T(8,128)(2,1)S(1)} %pad_maximum_fusion.3), channel_id=1, replica_groups=mesh['tile'=4,'rep'=8] {'tile'}, dimensions={1}, use_global_device_ids=true | all-gather | bytes 655360 | tf_op jit(solution)/shard_map/all_gather | solution.py:187
  28.4 1.7 maximum_maximum_fusion
  30.1 5.2 %fusion.72 = (f32[2,32,32]{2,1,0:T(8,128)S(1)}, f32[1,2,32,32,256]{4,3,2,1,0:T(8,128)S(1)}) fusion(f32[256]{0:T(256)S(1)} %bitcast.170, bf16[1,2,33,34,256]{4,3,2,1,0:T(8,128)(2,1)S(1)} %get-tuple-element.87, f32[256]{0:T(256)S(1)} %bitcast.172, f32[256]{0:T(256)S(1)} %bitcast.158, f32[256]{0:T(256)S(1)} %bitcast.160, ...), kind=kLoop, calls=%fused_computation.185 | loop fusion | flops 17299456 | bytes 9520128 | tf_op jit(solution)/shard_map/reduce_sum | solution.py:110
  36.8 19.3 %fusion.2 = (bf16[2048,1024]{1,0:T(8,128)(2,1)S(1)}, f32[2048,1024]{1,0:T(8,128)S(1)}) fusion(f32[1024]{0:T(1024)S(1)} %copy-done.13, bf16[2048,256]{1,0:T(8,128)(2,1)S(1)} %bitcast.144, bf16[256,1024]{1,0:T(8,128)(2,1)S(1)} %copy-done), kind=kOutput, calls=%fused_computation.8 | convolution fusion | flops 1212153856 | bytes 14159872 | tf_op jit(solution)/shard_map/dot_general | solution.py:115
  56.2 3.1 %fusion.58 = (f32[256]{0:T(256)}, bf16[2048,256]{1,0:T(8,128)(2,1)}, bf16[2048,256]{1,0:T(8,128)(2,1)S(1)}) fusion(bf16[1,2,32,32,256]{4,3,2,1,0:T(8,128)(2,1)S(1)} %copy-done.7, f32[256]{0:T(256)S(1)} %copy-done.14, bf16[1,2,32,32,256]{4,3,2,1,0:T(8,128)(2,1)S(1)} %copy-done.5, bf16[2048,1024]{1,0:T(8,128)(2,1)S(1)} %get-tuple-element.128, ...), kind=kOutput, calls=%fused_computation.102 | convolution fusion | flops 1078460160 | bytes 8914944 | tf_op jit(solution)/shard_map/dot_general | solution.py:117
  59.3 2.3 fusion.82
  61.6 5.5 %convert_reduce_fusion = (f32[1024]{0:T(1024)}, bf16[2048,1024]{1,0:T(8,128)(2,1)S(1)}) fusion(f32[2048,1024]{1,0:T(8,128)S(1)} %get-tuple-element.129, f32[1024]{0:T(1024)S(1)} %copy-done.13, bf16[2048,256]{1,0:T(8,128)(2,1)S(1)} %get-tuple-element.88, bf16[1024,256]{1,0:T(8,128)(2,1)S(1)} %copy-done.12), kind=kOutput, calls=%fused_computation.15 | convolution fusion | flops 1101003776 | bytes 14163968 | tf_op jit(solution)/shard_map/dot_general | solution.py:129
  67.0 1.9 copy-done.15
  69.0 2.2 fusion.81
  71.3 3.6 %multiply_reduce_fusion.3 = (f32[2048]{0:T(1024)S(1)}, f32[2048,256]{1,0:T(8,128)S(1)}) fusion(f32[256]{0:T(256)S(1)} %copy-done.9, bf16[2048,1024]{1,0:T(8,128)(2,1)} %copy-done.15, bf16[256,1024]{1,0:T(8,128)(2,1)S(1)} %copy-done), kind=kOutput, calls=%fused_computation.109 | convolution fusion | flops 1074788352 | bytes 6824960 | tf_op jit(solution)/shard_map/dot_general | solution.py:141
  74.9 1.1 multiply_reduce_fusion
  76.3 8.9 %fusion.48 = (f32[256]{0:T(256)S(1)}, f32[256]{0:T(256)}, f32[256]{0:T(256)}, f32[256]{0:T(256)}, f32[256]{0:T(256)}, /*index=5*/f32[256]{0:T(256)}, f32[256]{0:...) fusion(bf16[1,2,33,34,256]{4,3,2,1,0:T(8,128)(2,1)} %copy-done.2, ...), kind=kLoop, calls=%fused_computation.89 | loop fusion | flops 20969216 | bytes 13740032 | tf_op jit(solution)/shard_map/reduce_sum | solution.py:165
  85.2 2.7 %fusion.24 = f32[1,2,34,34,256]{4,3,2,1,0:T(8,128)S(1)} fusion(f32[1,2,32,32,256]{4,3,2,1,0:T(8,128)S(1)} %get-tuple-element.77, f32[256]{0:T(256)S(1)} %bitcast.171, f32[256]{0:T(256)S(1)} %bitcast.173, f32[256]{0:T(256)S(1)} %bitcast.159, f32[256]{0:T(256)S(1)} %bitcast.161, f32[256]{0:T(256)S(1)} %bitcast.163, f32[256]{0:T(256)S(1)} %bitcast.165, ...), kind=kLoop, calls=%fused_computation.48 | loop fusion | flops 10061824 | bytes 4473856 | tf_op jit(solution)/shard_map/add | solution.py:164
  88.7 1.0 copy-done.6
  90.1 7.3 %all_gather.14 = bf16[1,8,4,32,256]{4,3,2,0,1:T(8,128)(2,1)S(1)} all-gather(bf16[1,2,4,32,256]{4,3,2,0,1:T(8,128)(2,1)S(1)} %copy.228), channel_id=1, replica_groups=mesh['tile'=4,'rep'=8] {'tile'}, dimensions={1}, use_global_device_ids=true | all-gather | bytes 655360 | tf_op jit(solution)/shard_map/all_gather | solution.py:198
  97.3 1.1 bitcast_convert_fusion
  98.4 2.5 %gather_fusion.2 = f32[8,32,256]{2,1,0:T(8,128)} fusion(f32[8,4,32,256]{3,2,1,0:T(8,128)} %bitcast_convert_fusion, s32[8]{0:T(128)S(1)} %reshape.484), kind=kCustom, calls=%fused_computation.2 | custom fusion | bytes 524352 | tf_op jit(solution)/shard_map/gather | solution.py:37
  100.9 1.6 rev.37
  103.4 5.2 %all_gather.15 = bf16[1,8,4,256]{3,2,0,1:T(4,128)(2,1)S(1)} all-gather(bf16[1,2,4,256]{3,2,0,1:T(4,128)(2,1)S(1)} %copy.230), channel_id=1, replica_groups=mesh['tile'=4,'rep'=8] {'tile'}, dimensions={1}, use_global_device_ids=true | all-gather | bytes 20480 | tf_op jit(solution)/shard_map/all_gather | solution.py:201
  109.9 38.4 %all-reduce.1 = (f32[256,9]{0,1:T(8,128)S(1)}, f32[256]{0:T(256)S(1)}, f32[1024]{0:T(1024)S(1)}, f32[256]{0:T(256)S(1)}) all-reduce(f32[256,9]{0,1:T(8,128)S(1)} %stack.78, f32[256]{0:T(256)S(1)} %get-tuple-element.57, f32[1024]{0:T(1024)} %get-tuple-element.132, f32[256]{0:T(256)} %get-tuple-element.80), channel_id=1, replica_groups=mesh['tile'=4,'rep'=8] {'rep'}, use_global_device_ids=true, to_apply=%region_13.14 | all-reduce | flops 3840 | bytes 30720 | tf_op jit(solution)/shard_map/psum | solution.py:12
  148.3 10.6 %all-reduce.3 = (f32[256,9]{0,1:T(8,128)S(1)}, f32[256]{0:T(256)S(1)}, f32[1024]{0:T(1024)S(1)}, f32[256]{0:T(256)S(1)}) all-reduce(f32[256,9]{0,1:T(8,128)S(1)} %get-tuple-element.65, f32[256]{0:T(256)S(1)} %get-tuple-element.66, f32[1024]{0:T(1024)S(1)} %get-tuple-element.67, ...), channel_id=1, replica_groups=mesh['tile'=4,'rep'=8] {'tile'}, use_global_device_ids=true, to_apply=%region_14.15 | all-reduce | flops 3840 | bytes 30720 | tf_op jit(solution)/shard_map/psum | solution.py:13
  160.7 1.1 broadcast_select_fusion
  162.4 12.7 %all-reduce.8.cloned.1.call-done = (f32[256,1024]{1,0:T(8,128)}, f32[1024,256]{1,0:T(8,128)}) async-done(((f32[256,1024]{1,0:T(8,128)}, f32[1024,256]{1,0:T(8,128)}), (f32[256,1024]{1,0:T(8,128)}, f32[1024,256]{1,0:T(8,128)})) %all-reduce.8.cloned.1.call-update) | async-done | bytes 2097168 | tf_op jit(solution)/shard_map/psum | solution.py:12
  175.3 0.8 rev.39
  176.8 4.5 %fusion.56 = f32[1,2,32,32,256]{4,3,2,1,0:T(8,128)} fusion(f32[1,2,34,34,256]{4,3,2,1,0:T(8,128)S(1)} %fusion.24, bf16[1,2,32,32,256]{4,3,2,1,0:T(8,128)(2,1)} %param.11, f32[2,256]{1,0:T(2,128)S(1)} %bitcast.174, f32[2,256]{1,0:T(2,128)S(1)} %bitcast.175, f32[2,256]{1,0:T(2,128)S(1)} %bitcast.176, f32[2,256]{1,0:T(2,128)S(1)} %bitcast.177, ...), kind=kLoop, calls=%fused_computation.98 | loop fusion | flops 9437184 | bytes 5531648 | tf_op jit(solution)/shard_map/add | solution.py:93
  181.3 47.7 %all-reduce.10.cloned.1.call-done = (f32[256,1024]{1,0:T(8,128)}, f32[1024,256]{1,0:T(8,128)}) async-done(((f32[256,1024]{1,0:T(8,128)}, f32[1024,256]{1,0:T(8,128)}), (f32[256,1024]{1,0:T(8,128)}, f32[1024,256]{1,0:T(8,128)})) %all-reduce.10.cloned.1.call-update) | async-done | bytes 2097168 | tf_op jit(solution)/shard_map/psum | solution.py:13
  229.0 2.4 broadcast_multiply_fusion
  231.3 1.1 broadcast_multiply_fusion.1
  (105 shorter events, 12.4 us)
Async XLA Ops:
  7.2 29.6 %copy-start = (bf16[256,1024]{1,0:T(8,128)(2,1)S(1)}, bf16[256,1024]{1,0:T(8,128)(2,1)}, u32[]{:S(2)}) copy-start(bf16[256,1024]{1,0:T(8,128)(2,1)} %param.16) | copy-start | bytes 1572868
  7.2 21.2 %copy-start.4 = (bf16[1,2,32,32,256]{4,3,2,1,0:T(8,128)(2,1)S(1)}, bf16[1,2,32,32,256]{4,3,2,1,0:T(8,128)(2,1)}, u32[]{:S(2)}) copy-start(bf16[1,2,32,32,256]{4,3,2,1,0:T(8,128)(2,1)} %param.10) | copy-start | bytes 3145732
  7.2 21.1 %copy-start.10 = (f32[256,9]{0,1:T(8,128)S(1)}, f32[256,9]{0,1:T(8,128)}, u32[]{:S(2)}) copy-start(f32[256,9]{0,1:T(8,128)} %param.14) | copy-start | bytes 27652
  7.2 167.9 %all-reduce.8.cloned.1.call-start = ((), (), s32[]{:S(2)}) async-start(), calls=%async_computation | async-start | bytes 4194304 | tf_op jit(solution)/shard_map/psum | solution.py:12
  11.4 18.7 %copy-start.11 = (pred[2,4]{1,0:T(4,128)(4,1)}, pred[2,4]{1,0:T(4,128)(4,1)S(1)}, u32[]{:S(2)}) copy-start(pred[2,4]{1,0:T(4,128)(4,1)S(1)} %compare_bitcast_fusion) | copy-start | bytes 28
  30.1 5.2 %copy-start.1 = (bf16[1,2,33,34,256]{4,3,2,1,0:T(8,128)(2,1)}, bf16[1,2,33,34,256]{4,3,2,1,0:T(8,128)(2,1)S(1)}, u32[]{:S(2)}) copy-start(bf16[1,2,33,34,256]{4,3,2,1,0:T(8,128)(2,1)S(1)} %get-tuple-element.86) | copy-start | bytes 3446788
  30.1 5.2 %copy-start.2 = (bf16[1,2,33,34,256]{4,3,2,1,0:T(8,128)(2,1)}, bf16[1,2,33,34,256]{4,3,2,1,0:T(8,128)(2,1)S(1)}, u32[]{:S(2)}) copy-start(bf16[1,2,33,34,256]{4,3,2,1,0:T(8,128)(2,1)S(1)} %get-tuple-element.87) | copy-start | bytes 3446788
  30.1 5.9 %copy-start.9 = (f32[256]{0:T(256)S(1)}, f32[256]{0:T(256)}, u32[]{:S(2)}) copy-start(f32[256]{0:T(256)} %param.15) | copy-start | bytes 3076
  35.3 1.4 copy-start.13
  36.8 19.4 %copy-start.5 = (bf16[1,2,32,32,256]{4,3,2,1,0:T(8,128)(2,1)S(1)}, bf16[1,2,32,32,256]{4,3,2,1,0:T(8,128)(2,1)}, u32[]{:S(2)}) copy-start(bf16[1,2,32,32,256]{4,3,2,1,0:T(8,128)(2,1)} %param.10) | copy-start | bytes 3145732
  36.8 19.4 %copy-start.7 = (bf16[1,2,32,32,256]{4,3,2,1,0:T(8,128)(2,1)S(1)}, bf16[1,2,32,32,256]{4,3,2,1,0:T(8,128)(2,1)}, u32[]{:S(2)}) copy-start(bf16[1,2,32,32,256]{4,3,2,1,0:T(8,128)(2,1)} %param.11) | copy-start | bytes 3145732
  36.8 19.4 %copy-start.12 = (bf16[1024,256]{1,0:T(8,128)(2,1)S(1)}, bf16[1024,256]{1,0:T(8,128)(2,1)}, u32[]{:S(2)}) copy-start(bf16[1024,256]{1,0:T(8,128)(2,1)} %param.18) | copy-start | bytes 1572868
  36.8 19.4 %copy-start.14 = (f32[256]{0:T(256)S(1)}, f32[256]{0:T(256)}, u32[]{:S(2)}) copy-start(f32[256]{0:T(256)} %param.19) | copy-start | bytes 3076
  67.0 1.9 copy-start.15
  71.2 157.7 %all-reduce.10.cloned.1.call-start = ((), (), s32[]{:S(2)}) async-start(), calls=%async_computation.1 | async-start | bytes 4194304 | tf_op jit(solution)/shard_map/psum | solution.py:13
  74.9 1.3 copy-start.3
  88.6 1.1 copy-start.6
  228.9 2.4 copy-start.8
Sparse Core Ops, SparseCore 0:
  71.4 103.7 all-reduce.7
  177.6 51.3 all-reduce.9
